TPU v7x, 512 devices: a whole 4x8x8 slice. The times are simulated.
512 devices in a mesh: dp: 32 (over x, y_lo, core), tensor: 16 (over y_hi, z).
Axes of the slice: x: 4, y: 8 (y_hi: 2, y_lo: 4; y = y_hi * 4 + y_lo), z: 8, core: 2. Of those that a mesh axis runs over, the one named last changes fastest.
Arguments:
- layer_input: bfloat16 [32768, 4096], P('dp', 'tensor'), may hold values from -6 to 6
- up_grad: bfloat16 [32768, 14336], P('dp', 'tensor'), may hold values from -6 to 6
- hidden: bfloat16 [32768, 14336], P('dp', 'tensor'), may hold values from -6 to 6
- down_grad: bfloat16 [32768, 4096], P('dp', 'tensor'), may hold values from -6 to 6
- first_in: bfloat16 [4096, 64], P('tensor'), may hold values from -0.09375 to 0.09375
- first_out: bfloat16 [14336, 64], P('tensor'), may hold values from -0.046875 to 0.046875
- second_in: bfloat16 [14336, 64], P('tensor'), may hold values from -0.046875 to 0.046875
- second_out: bfloat16 [4096, 64], P('tensor'), may hold values from -0.09375 to 0.09375
- queries: bfloat16 [512, 8192], P('dp', 'tensor'), may hold values from -0.0078125 to 0.0078125
Outputs:
- scores: float32 [512, 512], P(('dp', 'tensor'))
All inputs are finite; a program needn't handle non-finite values.
Results may differ from a plain program's by a relative error of at most 0.014.
Values may be sent and summed in bfloat16 or wider, within the bound.
No kernel may reach another device: no remote copies, remote signals or barrier semaphores. Data moves between devices by JAX's collectives and lax.ppermute only.
A program may use at most 64 MiB of HBM per device.

v0:
```python
import jax
import jax.numpy as jnp
from jax import lax
from jax.sharding import PartitionSpec as P

K = 64
LEN = 64


def make_sketches(projected):
    seq_count = projected.shape[0] // LEN
    blocks = projected.reshape(seq_count, LEN, 4 * K)
    first = jnp.einsum("sti,stj->sij", blocks[:, :, K : 2 * K], blocks[:, :, 0:K]).reshape(
        seq_count, K * K
    )
    second = jnp.einsum("sti,stj->sij", blocks[:, :, 3 * K :], blocks[:, :, 2 * K : 3 * K]).reshape(
        seq_count, K * K
    )
    return jnp.concatenate([first, second], axis=1).astype(jnp.bfloat16)


def score_block(sketch, piece):
    return lax.dot_general(
        sketch, piece, (((1,), (1,)), ((), ())), preferred_element_type=jnp.float32
    )


def local(
    layer_input, up_grad, hidden, down_grad, first_in, first_out, second_in, second_out, queries
):
    projected = jnp.concatenate(
        [
            jnp.dot(layer_input, first_in, preferred_element_type=jnp.float32),
            jnp.dot(up_grad, first_out, preferred_element_type=jnp.float32),
            jnp.dot(hidden, second_in, preferred_element_type=jnp.float32),
            jnp.dot(down_grad, second_out, preferred_element_type=jnp.float32),
        ],
        axis=1,
    )
    shares = lax.psum_scatter(projected, "tensor", scatter_dimension=0, tiled=True)
    sketch = make_sketches(shares)
    columns = lax.all_gather(queries, "tensor", axis=1, tiled=True)
    return score_block(sketch, lax.all_gather(columns, "dp", axis=0, tiled=True))


def solution(mesh):
    placed = (
        P("dp", "tensor"),
        P("dp", "tensor"),
        P("dp", "tensor"),
        P("dp", "tensor"),
        P("tensor", None),
        P("tensor", None),
        P("tensor", None),
        P("tensor", None),
        P("dp", "tensor"),
    )
    return jax.shard_map(
        local, mesh=mesh, in_specs=placed, out_specs=P(("dp", "tensor"), None), check_vma=False
    )
```

profile of v0, /device:TPU:4, one launch (start us, length us, event | category | flops | bytes accessed | tf_op | source)
XLA Modules:
  0.0 254.1 jit_solution(3393536245409682924)
XLA Ops:
  7.4 0.0 copy-start
  7.4 0.0 copy-start.3
  7.4 0.0 reduce-scatter.4.cloned.1.call-start
  7.4 0.0 copy-start.1
  7.4 1.5 fusion
  8.8 0.2 copy-done
  9.0 0.0 copy-start.2
  9.0 0.0 copy-start.4
  9.0 1.6 fusion.1
  10.7 0.0 copy-done.3
  10.7 0.0 copy-done.1
  10.7 0.7 fusion.2
  11.4 0.0 copy-done.2
  11.4 0.0 copy-done.4
  11.4 0.3 fusion.3
  11.7 0.1 pad_maximum_fusion
  11.8 0.0 copy-start.5
  11.8 1.4 copy.10
  13.2 0.0 reduce-scatter.4.cloned.1.call-update
  13.2 0.0 all-gather.2.cloned.1.call-start
  13.2 0.0 copy-done.5
  13.2 63.3 %all_gather.6 = bf16[16,8192]{1,0:T(8,128)(2,1)} all-gather(bf16[16,512]{1,0:T(8,128)(2,1)S(1)} %copy-done.5), channel_id=1, replica_groups=mesh['dp'=32,'tensor'=16] {'tensor'}, dimensions={1}, use_global_device_ids=true | all-gather | bytes 278528 | tf_op jit(solution)/shard_map/all_gather | solution.py:42
  76.6 0.0 all-gather.2.cloned.1.call-update
  76.6 162.4 %reduce-scatter.4.cloned.1.call-done = f32[64,256]{1,0:T(8,128)} async-done(((f32[1024,256]{1,0:T(8,128)}), f32[64,256]{1,0:T(8,128)}) %reduce-scatter.4.cloned.1.call-update) | async-done | bytes 65552
  239.0 0.9 copy.11
  239.9 0.1 convolution_convert_fusion
  240.0 0.1 concatenate.16
  240.1 0.1 convolution_convert_fusion.1
  240.3 0.1 concatenate.15
  240.4 0.0 all-gather.2.cloned.1.call-done
  240.4 6.2 %fusion.4 = f32[1,512]{1,0:T(1,128)} fusion(bf16[8192,1]{0,1:T(2,128)(2,1)S(1)} %reshape.43, bf16[512,8192]{1,0:T(8,128)(2,1)} %all-gather.2.cloned.1.call-done), kind=kOutput, calls=%fused_computation.12 | convolution fusion | flops 8388608 | bytes 8407040 | tf_op jit(solution)/shard_map/dot_general | solution.py:23
  (2 shorter events, 0.0 us)
Async XLA Ops:
  7.4 1.7 copy-start
  7.4 3.3 %copy-start.3 = (bf16[896,64]{0,1:T(8,128)(2,1)S(1)}, bf16[896,64]{0,1:T(8,128)(2,1)}, u32[]{:S(2)}) copy-start(bf16[896,64]{0,1:T(8,128)(2,1)} %param.15) | copy-start | bytes 344068
  7.4 231.6 %reduce-scatter.4.cloned.1.call-start = ((), (), s32[]{:S(2)}) async-start(), calls=%async_computation.2 | async-start | bytes 1114112
  7.4 3.3 %copy-start.1 = (bf16[1024,896]{1,0:T(8,128)(2,1)S(1)}, bf16[1024,896]{1,0:T(8,128)(2,1)}, u32[]{:S(2)}) copy-start(bf16[1024,896]{1,0:T(8,128)(2,1)} %param.11) | copy-start | bytes 5505028
  9.0 2.3 copy-start.2
  9.0 2.3 copy-start.4
  11.8 1.5 copy-start.5
  13.2 227.2 %all-gather.2.cloned.1.call-start = ((), (), s32[]{:S(2)}) async-start(), calls=%async_computation.1 | async-start | bytes 8650752 | tf_op jit(solution)/shard_map/all_gather | solution.py:43
Sparse Core Ops, SparseCore 0:
  13.3 225.6 reduce-scatter.3
Sparse Core Ops, SparseCore 1:
  76.7 63.9 all-gather.1
where the time goes:
time: 254 us
  waiting for transfers between devices  162 us (64%)
  blocking collectives  63.3 us (25%)
  between operations  14.9 us (6%)
  matrix products  10.5 us (4%)
  local copies, waits for them, and re-layouts  2.78 us (1%)
    unnamed x3, waiting for transfers between devices  162 us
    all_gather x1, blocking collectives, local(): columns = lax.all_gather(queries, 'tensor', axis=1, tiled=True)  63.3 us
    dot_general x1, matrix products, score_block(): lax.dot_general(sketch, piece, (((1,), (1,)), ((), ())), preferred_elemen...  6.23 us
  transfers between devices with their start and end apart: 2, of which 1 were waited for; matrix products, arithmetic and copies ran while one was open for 1% of the time, Pallas kernels for 0%

commit v1 on v0

v1 whole, which is shorter than its diff:
```python
import jax
import jax.numpy as jnp
from jax import lax
from jax.sharding import PartitionSpec as P

K = 64
LEN = 64
T = ("yh", "z")
D = ("x", "yl", "c")


def local(
    layer_input, up_grad, hidden, down_grad, first_in, first_out, second_in, second_out, queries
):
    rows, width = queries.shape
    copies = jnp.broadcast_to(queries[None], (8, rows, width))
    q = lax.all_to_all(copies, ("yh", "yl"), 0, 0, tiled=True).reshape(2, 4, rows, width)
    pieces = [
        jnp.dot(x, w, preferred_element_type=jnp.float32).astype(jnp.bfloat16)
        for x, w in (
            (layer_input, first_in),
            (up_grad, first_out),
            (hidden, second_in),
            (down_grad, second_out),
        )
    ]
    projected = jnp.concatenate(pieces, axis=1).reshape(16, LEN, 4 * K)
    projected, q = lax.optimization_barrier((projected, q))
    shares = lax.all_to_all(projected, T, 0, 0, tiled=True)
    q = lax.all_gather(q, "x", axis=0)
    halves = [lax.all_gather(q[:, h], "c", axis=0).reshape(32 * rows, width) for h in range(2)]
    p = jnp.sum(shares.astype(jnp.float32), axis=0)
    sketch = jnp.stack(
        [
            lax.dot_general(b, a, (((0,), (0,)), ((), ())), preferred_element_type=jnp.float32)
            .astype(jnp.bfloat16)
            .reshape(8, width)
            for a, b in (
                (p[:, 0:K], p[:, K : 2 * K]),
                (p[:, 2 * K : 3 * K], p[:, 3 * K :]),
            )
        ],
        axis=1,
    )
    sketch = lax.all_to_all(sketch, "z", 0, 0, tiled=True)
    part = sum(
        lax.dot_general(
            sketch[:, h], halves[h], (((1,), (1,)), ((), ())), preferred_element_type=jnp.float32
        )
        for h in range(2)
    )
    part = lax.all_to_all(part, "z", 0, 0, tiled=True)
    row = jnp.sum(part, axis=0).reshape(2, 16, rows)
    return jnp.transpose(row, (1, 0, 2)).reshape(1, 32 * rows)


def solution(mesh):
    fine = jax.sharding.Mesh(mesh.devices.reshape(4, 4, 2, 2, 8), D + T)
    placed = (P(D, T),) * 4 + (P(T, None),) * 4 + (P(D, T),)
    return jax.shard_map(
        local, mesh=fine, in_specs=placed, out_specs=P(D + T, None), check_vma=False
    )
```

time: 254 us -> 75.2 us (0.30)
  the two profiles are of different devices: /device:TPU:4 before, /device:TPU:10 now
where the time goes in v1:
time: 75.2 us; the launch traced here: 74.7 us
  blocking collectives  27.7 us (37%)
  starting transfers between devices  24.7 us (33%)
  waiting for transfers between devices  12.8 us (17%)
  matrix products  5.02 us (7%)
  local copies, waits for them, and re-layouts  3.56 us (5%)
  other arithmetic  0.78 us (1%)
    all_gather x1, blocking collectives, local(): q = lax.all_gather(q, 'x', axis=0)  13.2 us
    all_to_all x1, starting transfers between devices, local(): shares = lax.all_to_all(projected, T, 0, 0, tiled=True)  12.1 us
    all_to_all x1, blocking collectives, local(): part = lax.all_to_all(part, 'z', 0, 0, tiled=True)  10.1 us
    all_to_all x1, starting transfers between devices, local(): lax.all_to_all(copies, ('yh', 'yl'), 0, 0, tiled=True)  7.55 us
    all_to_all x1, waiting for transfers between devices, local(): sketch = lax.all_to_all(sketch, 'z', 0, 0, tiled=True)  5.6 us
    all_to_all x1, starting transfers between devices, local(): sketch = lax.all_to_all(sketch, 'z', 0, 0, tiled=True)  5.09 us
    all_to_all x1, waiting for transfers between devices, local(): shares = lax.all_to_all(projected, T, 0, 0, tiled=True)  4.95 us
    all_gather x2, blocking collectives, local(): lax.all_gather(q[:, h], 'c', axis=0).reshape(32 * rows, width)  4.35 us
  transfers between devices with their start and end apart: 3, of which 3 were waited for; matrix products, arithmetic and copies ran while one was open for 7% of the time, Pallas kernels for 0%

profile of v1, /device:TPU:10, one launch (start us, length us, event | category | flops | bytes accessed | tf_op | source)
XLA Modules:
  0.0 74.7 jit_solution(8137370535523127665)
XLA Ops:
  0.0 0.0 copy-start
  0.0 1.5 %broadcast_in_dim.2 = bf16[8,16,512]{2,1,0:T(8,128)(2,1)} broadcast(bf16[16,512]{1,0:T(8,128)(2,1)} %param.17), dimensions={1,2} | broadcast | bytes 147456 | tf_op jit(solution)/shard_map/broadcast_in_dim | solution.py:16
  1.5 7.5 %all-to-all-start = ((bf16[8,16,512]{2,1,0:T(8,128)(2,1)}), bf16[8,16,512]{2,1,0:T(8,128)(2,1)S(1)}, u32[]{:S(2)}, u32[]{:S(2)}) async-start(bf16[8,16,512]{2,1,0:T(8,128)(2,1)} %broadcast_in_dim.2), calls=%async_computation | async-start | bytes 262144 | tf_op jit(solution)/shard_map/all_to_all | solution.py:17
  9.1 1.5 %convolution_convert_fusion = bf16[1024,64]{0,1:T(8,128)(2,1)S(1)} fusion(bf16[1024,256]{1,0:T(8,128)(2,1)} %param.12, bf16[256,64]{0,1:T(8,128)(2,1)} %param.16), kind=kOutput, calls=%fused_computation | convolution fusion | flops 33619968 | bytes 688128 | tf_op jit(solution)/shard_map/dot_general | solution.py:19
  10.5 0.0 copy-done
  10.5 0.0 copy-start.2
  10.5 0.0 copy-start.4
  10.5 1.6 %convolution_convert_fusion.2 = bf16[1024,64]{0,1:T(8,128)(2,1)S(1)} fusion(bf16[1024,896]{1,0:T(8,128)(2,1)S(1)} %copy-done, bf16[896,64]{0,1:T(8,128)(2,1)} %param.15), kind=kOutput, calls=%fused_computation.2 | convolution fusion | flops 117506048 | bytes 2080768 | tf_op jit(solution)/shard_map/dot_general | solution.py:19
  12.2 0.0 copy-done.3
  12.2 0.0 copy-done.1
  12.2 0.7 convolution_convert_fusion.3
  12.9 0.3 convolution_convert_fusion.1
  13.2 1.0 %copy.18 = bf16[1024,256]{1,0:T(8,128)(2,1)} copy(bf16[1024,256]{0,1:T(8,128)(2,1)S(1)} %pad_maximum_fusion) | data formatting | bytes 1048576 | tf_op jit(solution)/shard_map/concatenate | solution.py:27
  14.2 2.3 %all-to-all-done = bf16[8,16,512]{2,1,0:T(8,128)(2,1)S(1)} async-done(((bf16[8,16,512]{2,1,0:T(8,128)(2,1)}), bf16[8,16,512]{2,1,0:T(8,128)(2,1)S(1)}, u32[]{:S(2)}, u32[]{:S(2)}) %all-to-all-start) | async-done | bytes 131104 | tf_op jit(solution)/shard_map/all_to_all | solution.py:17
  16.5 12.1 %all-to-all-start.1 = ((bf16[16,64,256]{2,1,0:T(8,128)(2,1)}), bf16[16,64,256]{2,1,0:T(8,128)(2,1)S(1)}, u32[]{:S(2)}, u32[]{:S(2)}) async-start(bf16[16,64,256]{2,1,0:T(8,128)(2,1)} %bitcast), calls=%async_computation.1 | async-start | bytes 1048576 | tf_op jit(solution)/shard_map/all_to_all | solution.py:29
  28.6 13.2 %all-gather = bf16[8,4,16,512]{3,2,1,0:T(8,128)(2,1)S(1)} all-gather(bf16[2,4,16,512]{3,2,1,0:T(8,128)(2,1)S(1)} %bitcast.27), channel_id=2, replica_groups=mesh['x'=4,'yl'=4,'c'=2,'yh'=2,'z'=8] {'x'}, dimensions={0}, use_global_device_ids=true | all-gather | bytes 655360 | tf_op jit(solution)/shard_map/all_gather | solution.py:30
  41.9 2.2 %all-gather.1 = bf16[8,1,4,16,512]{4,3,2,1,0:T(8,128)(2,1)S(1)} all-gather(bf16[4,1,4,16,512]{4,3,2,1,0:T(8,128)(2,1)S(1)} %get-tuple-element.10), channel_id=3, replica_groups=mesh['x'=4,'yl'=4,'c'=2,'yh'=2,'z'=8] {'c'}, dimensions={0}, use_global_device_ids=true | all-gather | bytes 786432 | tf_op jit(solution)/shard_map/all_gather | solution.py:31
  44.0 4.9 %all-to-all-done.1 = bf16[16,64,256]{2,1,0:T(8,128)(2,1)S(1)} async-done(((bf16[16,64,256]{2,1,0:T(8,128)(2,1)}), bf16[16,64,256]{2,1,0:T(8,128)(2,1)S(1)}, u32[]{:S(2)}, u32[]{:S(2)}) %all-to-all-start.1) | async-done | bytes 524320 | tf_op jit(solution)/shard_map/all_to_all | solution.py:29
  49.0 0.1 convert_reduce_fusion
  49.1 0.2 convolution_convert_fusion.5
  49.3 0.2 convolution_convert_fusion.4
  49.6 0.1 stack_reshape.8
  49.6 0.1 stack_reshape.9
  49.7 0.6 pad_maximum_fusion.1
  50.4 5.1 %all-to-all-start.2 = ((bf16[8,2,512]{2,1,0:T(2,128)(2,1)}), bf16[8,2,512]{2,1,0:T(2,128)(2,1)S(1)}, u32[]{:S(2)}, u32[]{:S(2)}) async-start(bf16[8,2,512]{2,1,0:T(2,128)(2,1)} %pad_maximum_fusion.1), calls=%async_computation.2 | async-start | bytes 32768 | tf_op jit(solution)/shard_map/all_to_all | solution.py:45
  55.5 2.2 %all-gather.2 = bf16[8,1,4,16,512]{4,3,2,1,0:T(8,128)(2,1)S(1)} all-gather(bf16[4,1,4,16,512]{4,3,2,1,0:T(8,128)(2,1)S(1)} %get-tuple-element.9), channel_id=4, replica_groups=mesh['x'=4,'yl'=4,'c'=2,'yh'=2,'z'=8] {'c'}, dimensions={0}, use_global_device_ids=true | all-gather | bytes 786432 | tf_op jit(solution)/shard_map/all_gather | solution.py:31
  57.6 5.6 %all-to-all-done.2 = bf16[8,2,512]{2,1,0:T(2,128)(2,1)S(1)} async-done(((bf16[8,2,512]{2,1,0:T(2,128)(2,1)}), bf16[8,2,512]{2,1,0:T(2,128)(2,1)S(1)}, u32[]{:S(2)}, u32[]{:S(2)}) %all-to-all-start.2) | async-done | bytes 16416 | tf_op jit(solution)/shard_map/all_to_all | solution.py:45
  63.3 0.2 fusion.5
  63.5 0.3 fusion
  63.8 10.1 %all_to_all.24 = f32[8,1,512]{2,1,0:T(1,128)S(1)} all-to-all(f32[8,1,512]{2,1,0:T(1,128)S(1)} %copy.23), channel_id=1, replica_groups=mesh['x'=4,'yl'=4,'c'=2,'yh'=2,'z'=8] {'z'}, dimensions={0} | all-to-all | bytes 32768 | tf_op jit(solution)/shard_map/all_to_all | solution.py:52
  74.0 0.1 reshape.25
  74.1 0.7 reshape.26
  (10 shorter events, 0.2 us)
Async XLA Ops:
  0.0 10.5 %copy-start = (bf16[1024,896]{1,0:T(8,128)(2,1)S(1)}, bf16[1024,896]{1,0:T(8,128)(2,1)}, u32[]{:S(2)}) copy-start(bf16[1024,896]{1,0:T(8,128)(2,1)} %param.11) | copy-start | bytes 5505028
  0.0 12.2 %copy-start.3 = (bf16[896,64]{0,1:T(8,128)(2,1)S(1)}, bf16[896,64]{0,1:T(8,128)(2,1)}, u32[]{:S(2)}) copy-start(bf16[896,64]{0,1:T(8,128)(2,1)} %param.14) | copy-start | bytes 344068
  1.5 15.0 %all-to-all-start = ((bf16[8,16,512]{2,1,0:T(8,128)(2,1)}), bf16[8,16,512]{2,1,0:T(8,128)(2,1)S(1)}, u32[]{:S(2)}, u32[]{:S(2)}) async-start(bf16[8,16,512]{2,1,0:T(8,128)(2,1)} %broadcast_in_dim.2), calls=%async_computation | async-start | bytes 262144 | tf_op jit(solution)/shard_map/all_to_all | solution.py:17
  9.1 3.1 %copy-start.1 = (bf16[1024,896]{1,0:T(8,128)(2,1)S(1)}, bf16[1024,896]{1,0:T(8,128)(2,1)}, u32[]{:S(2)}) copy-start(bf16[1024,896]{1,0:T(8,128)(2,1)} %param.10) | copy-start | bytes 5505028
  10.5 2.4 %copy-start.2 = (bf16[1024,256]{1,0:T(8,128)(2,1)S(1)}, bf16[1024,256]{1,0:T(8,128)(2,1)}, u32[]{:S(2)}) copy-start(bf16[1024,256]{1,0:T(8,128)(2,1)} %param.9) | copy-start | bytes 1572868
  10.5 2.4 %copy-start.4 = (bf16[256,64]{0,1:T(8,128)(2,1)S(1)}, bf16[256,64]{0,1:T(8,128)(2,1)}, u32[]{:S(2)}) copy-start(bf16[256,64]{0,1:T(8,128)(2,1)} %param.13) | copy-start | bytes 98308
  16.5 32.5 %all-to-all-start.1 = ((bf16[16,64,256]{2,1,0:T(8,128)(2,1)}), bf16[16,64,256]{2,1,0:T(8,128)(2,1)S(1)}, u32[]{:S(2)}, u32[]{:S(2)}) async-start(bf16[16,64,256]{2,1,0:T(8,128)(2,1)} %bitcast), calls=%async_computation.1 | async-start | bytes 1048576 | tf_op jit(solution)/shard_map/all_to_all | solution.py:29
  50.4 12.9 %all-to-all-start.2 = ((bf16[8,2,512]{2,1,0:T(2,128)(2,1)}), bf16[8,2,512]{2,1,0:T(2,128)(2,1)S(1)}, u32[]{:S(2)}, u32[]{:S(2)}) async-start(bf16[8,2,512]{2,1,0:T(2,128)(2,1)} %pad_maximum_fusion.1), calls=%async_computation.2 | async-start | bytes 32768 | tf_op jit(solution)/shard_map/all_to_all | solution.py:45

commit v2 on v1

v2 whole, which is shorter than its diff:
```python
import jax
import jax.numpy as jnp
from jax import lax
from jax.experimental import pallas as pl
from jax.experimental.pallas import tpu as pltpu
from jax.sharding import PartitionSpec as P

K = 64
LEN = 64
T = ("yh", "z")
D = ("x", "yl", "c")
WHOLE = pl.BlockSpec(memory_space=pltpu.VMEM)
F32 = jnp.float32
BF16 = jnp.bfloat16


def project_kernel(x0, x1, x2, x3, w0, w1, w2, w3, out):
    def layer(xa, xb, wa, wb):
        x = jnp.concatenate([xa[...], xb[...]], axis=1)
        w = jnp.concatenate(
            [
                jnp.concatenate([wa[...], jnp.zeros(wb.shape, BF16)], axis=1),
                jnp.concatenate([jnp.zeros(wa.shape, BF16), wb[...]], axis=1),
            ],
            axis=0,
        )
        return lax.dot_general(x, w, (((1,), (1,)), ((), ())), preferred_element_type=F32)

    both = jnp.concatenate([layer(x0, x1, w0, w1), layer(x2, x3, w2, w3)], axis=1)
    out[...] = both.astype(BF16).reshape(out.shape)


def project(xs, ws):
    rows = 512
    xs = [pltpu.with_memory_space_constraint(x, pltpu.HBM) for x in xs]
    ws = [pltpu.with_memory_space_constraint(w.T, pltpu.HBM) for w in ws]
    return pl.pallas_call(
        project_kernel,
        out_shape=jax.ShapeDtypeStruct((16, LEN, 4 * K), BF16),
        grid=(xs[0].shape[0] // rows,),
        in_specs=[pl.BlockSpec((rows, x.shape[1]), lambda i: (i, 0)) for x in xs]
        + [pl.BlockSpec(w.shape, lambda i: (0, 0)) for w in ws],
        out_specs=pl.BlockSpec((rows // LEN, LEN, 4 * K), lambda i: (i, 0, 0)),
        compiler_params=pltpu.CompilerParams(vmem_limit_bytes=40 << 20),
        name="project",
    )(*xs, *ws)


def sketches(shares):
    p = jnp.sum(shares.astype(F32), axis=0)
    return jnp.stack(
        [
            lax.dot_general(p[:, s + K : s + 2 * K], p[:, s : s + K], (((0,), (0,)), ((), ())), preferred_element_type=F32)
            .astype(BF16)
            .reshape(8, 8 * K)
            for s in (0, 2 * K)
        ],
        axis=1,
    )


def score_kernel(sketch, *refs):
    pieces, out = refs[:-1], refs[-1]
    me = lax.axis_index("x")
    for k, piece in enumerate(pieces):
        total = None
        for l in range(2):
            rows = jnp.concatenate([piece[c, l, y] for y in range(4) for c in range(2)], axis=0)
            part = lax.dot_general(sketch[:, l, :], rows, (((1,), (1,)), ((), ())), preferred_element_type=F32)
            total = part if total is None else total + part
        at = lax.rem(me + 4 - k, 4) * 128
        out[:, pl.ds(pl.multiple_of(at, 128), 128)] = total


def score(sketch, pieces):
    return pl.pallas_call(
        score_kernel,
        out_shape=jax.ShapeDtypeStruct((8, 512), F32),
        in_specs=[WHOLE] * (1 + len(pieces)),
        out_specs=WHOLE,
        compiler_params=pltpu.CompilerParams(vmem_limit_bytes=16 << 20),
        name="score",
    )(sketch, *pieces)


def local(layer_input, up_grad, hidden, down_grad, first_in, first_out, second_in, second_out, queries):
    rows, width = queries.shape
    copies = jnp.broadcast_to(queries[None], (8, rows, width))
    q = lax.all_to_all(copies, ("yh", "yl"), 0, 0, tiled=True).reshape(2, 4, rows, width)
    projected = project((layer_input, up_grad, hidden, down_grad), (first_in, first_out, second_in, second_out))
    projected, q = lax.optimization_barrier((projected, q))
    shares = lax.all_to_all(projected, T, 0, 0, tiled=True)
    q = lax.all_gather(q, "c", axis=0)
    pieces = [q] + [lax.ppermute(q, "x", [(i, (i + k) % 4) for i in range(4)]) for k in (1, 3, 2)]
    pieces = [pieces[0], pieces[1], pieces[3], pieces[2]]
    sketch = lax.all_to_all(sketches(shares), "z", 0, 0, tiled=True)
    part = score(sketch, pieces)
    part = lax.all_to_all(part, "z", 0, 0, tiled=True)
    return jnp.sum(part, axis=0, keepdims=True)


def solution(mesh):
    fine = jax.sharding.Mesh(mesh.devices.reshape(4, 4, 2, 2, 8), D + T)
    placed = (P(D, T),) * 4 + (P(T, None),) * 4 + (P(D, T),)
    return jax.shard_map(local, mesh=fine, in_specs=placed, out_specs=P(D + T, None), check_vma=False)
```

time: 75.2 us -> 72.9 us (0.969)
  the two profiles are of different devices: /device:TPU:10 before, /device:TPU:22 now
where the time goes in v2:
time: 72.9 us; the launch traced here: 72.3 us
  starting transfers between devices  34.2 us (47%)
  waiting for transfers between devices  17.9 us (25%)
  blocking collectives  12.1 us (17%)
  Pallas kernels  4.55 us (6%)
  local copies, waits for them, and re-layouts  1.59 us (2%)
  other arithmetic  1.33 us (2%)
    all_to_all x1, starting transfers between devices, local(): shares = lax.all_to_all(projected, T, 0, 0, tiled=True)  12.6 us
    all_to_all x1, blocking collectives, local(): part = lax.all_to_all(part, 'z', 0, 0, tiled=True)  10.1 us
    ppermute x3, starting transfers between devices, local(): lax.ppermute(q, 'x', [(i, (i + k) % 4) for i in range(4)])  9.75 us
    all_to_all x1, waiting for transfers between devices, local(): shares = lax.all_to_all(projected, T, 0, 0, tiled=True)  8.19 us
    all_to_all x1, waiting for transfers between devices, local(): sketch = lax.all_to_all(sketches(shares), 'z', 0, 0, tiled=True)  7.75 us
    all_to_all x1, starting transfers between devices, local(): lax.all_to_all(copies, ('yh', 'yl'), 0, 0, tiled=True)  7.43 us
    all_to_all x1, starting transfers between devices, local(): sketch = lax.all_to_all(sketches(shares), 'z', 0, 0, tiled=True)  4.46 us
    pallas_call x1, Pallas kernels, project(): pl.pallas_call(project_kernel, out_shape=jax.ShapeDtypeStruct((16, LEN, 4...  4.2 us
  transfers between devices with their start and end apart: 6, of which 3 were waited for; matrix products, arithmetic and copies ran while one was open for 2% of the time, Pallas kernels for 6%

profile of v2, /device:TPU:22, one launch (start us, length us, event | category | flops | bytes accessed | tf_op | source)
XLA Modules:
  0.0 72.3 jit_solution(11601324941777816234)
XLA Ops:
  0.0 1.4 %broadcast_in_dim.4 = bf16[8,16,512]{2,1,0:T(8,128)(2,1)} broadcast(bf16[16,512]{1,0:T(8,128)(2,1)} %param.17), dimensions={1,2} | broadcast | bytes 147456 | tf_op jit(solution)/shard_map/broadcast_in_dim | solution.py:88
  1.4 7.4 %all-to-all-start = ((bf16[8,16,512]{2,1,0:T(8,128)(2,1)}), bf16[8,16,512]{2,1,0:T(8,128)(2,1)S(1)}, u32[]{:S(2)}, u32[]{:S(2)}) async-start(bf16[8,16,512]{2,1,0:T(8,128)(2,1)} %broadcast_in_dim.4), calls=%async_computation | async-start | bytes 262144 | tf_op jit(solution)/shard_map/all_to_all | solution.py:89
  8.8 4.2 %project.1 = bf16[16,64,256]{2,1,0:T(8,128)(2,1)} custom-call(bf16[1024,256]{1,0:T(8,128)(2,1)} %x0.1, bf16[1024,896]{1,0:T(8,128)(2,1)} %x1.1, bf16[1024,896]{1,0:T(8,128)(2,1)} %x2.1, bf16[1024,256]{1,0:T(8,128)(2,1)} %x3.1, bf16[64,256]{1,0:T(8,128)(2,1)} %bitcast.16, bf16[64,896]{1,0:T(8,128)(2,1)} %bitcast.14, bf16[64,896]{1,0:T(8,128)(2,1)} %bitcast.15, ...), custom_call_target="tpu_custom_call" | custom-call | tf_op jit(solution)/shard_map/project/pallas_call | solution.py:37
  13.0 2.0 %all-to-all-done = bf16[8,16,512]{2,1,0:T(8,128)(2,1)S(1)} async-done(((bf16[8,16,512]{2,1,0:T(8,128)(2,1)}), bf16[8,16,512]{2,1,0:T(8,128)(2,1)S(1)}, u32[]{:S(2)}, u32[]{:S(2)}) %all-to-all-start) | async-done | bytes 131104 | tf_op jit(solution)/shard_map/all_to_all | solution.py:89
  15.0 12.6 %all-to-all-start.1 = ((bf16[16,64,256]{2,1,0:T(8,128)(2,1)}), bf16[16,64,256]{2,1,0:T(8,128)(2,1)S(1)}, u32[]{:S(2)}, u32[]{:S(2)}) async-start(bf16[16,64,256]{2,1,0:T(8,128)(2,1)} %project.1), calls=%async_computation.1 | async-start | bytes 1048576 | tf_op jit(solution)/shard_map/all_to_all | solution.py:92
  27.6 2.0 %all-gather = bf16[4,4,16,512]{3,2,1,0:T(8,128)(2,1)S(1)} all-gather(bf16[2,4,16,512]{3,2,1,0:T(8,128)(2,1)S(1)} %bitcast.13), channel_id=2, replica_groups=mesh['x'=4,'yl'=4,'c'=2,'yh'=2,'z'=8] {'c'}, dimensions={0}, use_global_device_ids=true | all-gather | bytes 393216 | tf_op jit(solution)/shard_map/all_gather | solution.py:93
  29.6 2.7 %collective-permute-start.2 = (bf16[2,2,4,16,512]{4,3,2,1,0:T(8,128)(2,1)S(1)}, bf16[2,2,4,16,512]{4,3,2,1,0:T(8,128)(2,1)S(1)}, u32[]{:S(2)}, u32[]{:S(2)}) collective-permute-start(bf16[2,2,4,16,512]{4,3,2,1,0:T(8,128)(2,1)S(1)} %bitcast.8), channel_id=1, source_target_pairs={{0,384},{128,0},{256,128},{384,256},{1,385},{129,1},{257,129},{385... | collective-permute-start | bytes 786440 | tf_op jit(solution)/shard_map/ppermute | solution.py:94
  32.3 3.0 %collective-permute-start.1 = (bf16[2,2,4,16,512]{4,3,2,1,0:T(8,128)(2,1)S(1)}, bf16[2,2,4,16,512]{4,3,2,1,0:T(8,128)(2,1)S(1)}, u32[]{:S(2)}, u32[]{:S(2)}) collective-permute-start(bf16[2,2,4,16,512]{4,3,2,1,0:T(8,128)(2,1)S(1)} %bitcast.9), channel_id=1, source_target_pairs={{0,256},{128,384},{256,0},{384,128},{1,257},{129,385},{257,1},{385... | collective-permute-start | bytes 786440 | tf_op jit(solution)/shard_map/ppermute | solution.py:94
  35.3 4.0 %collective-permute-start = (bf16[2,2,4,16,512]{4,3,2,1,0:T(8,128)(2,1)S(1)}, bf16[2,2,4,16,512]{4,3,2,1,0:T(8,128)(2,1)S(1)}, u32[]{:S(2)}, u32[]{:S(2)}) collective-permute-start(bf16[2,2,4,16,512]{4,3,2,1,0:T(8,128)(2,1)S(1)} %bitcast.10), channel_id=1, source_target_pairs={{0,128},{128,256},{256,384},{384,0},{1,129},{129,257},{257,385},{3... | collective-permute-start | bytes 786440 | tf_op jit(solution)/shard_map/ppermute | solution.py:94
  39.4 8.2 %all-to-all-done.1 = bf16[16,64,256]{2,1,0:T(8,128)(2,1)S(1)} async-done(((bf16[16,64,256]{2,1,0:T(8,128)(2,1)}), bf16[16,64,256]{2,1,0:T(8,128)(2,1)S(1)}, u32[]{:S(2)}, u32[]{:S(2)}) %all-to-all-start.1) | async-done | bytes 524320 | tf_op jit(solution)/shard_map/all_to_all | solution.py:92
  47.5 0.1 convert_reduce_fusion
  47.6 0.2 convolution_convert_fusion
  47.9 0.1 stack_reshape.9
  48.0 0.2 convolution_convert_fusion.1
  48.2 0.1 stack_reshape.8
  48.3 0.7 pad_maximum_fusion
  48.9 4.5 %all-to-all-start.2 = ((bf16[8,2,512]{2,1,0:T(2,128)(2,1)}), bf16[8,2,512]{2,1,0:T(2,128)(2,1)S(1)}, u32[]{:S(2)}, u32[]{:S(2)}) async-start(bf16[8,2,512]{2,1,0:T(2,128)(2,1)} %pad_maximum_fusion), calls=%async_computation.2 | async-start | bytes 32768 | tf_op jit(solution)/shard_map/all_to_all | solution.py:96
  53.4 0.0 collective-permute-done.2.refs_3_
  53.4 0.0 collective-permute-done.1.refs_2_
  53.4 0.0 collective-permute-done.refs_1_
  53.4 7.7 %all-to-all-done.2.sketch = bf16[8,2,512]{2,1,0:T(2,128)(2,1)S(1)} async-done(((bf16[8,2,512]{2,1,0:T(2,128)(2,1)}), bf16[8,2,512]{2,1,0:T(2,128)(2,1)S(1)}, u32[]{:S(2)}, u32[]{:S(2)}) %all-to-all-start.2) | async-done | bytes 16416 | tf_op jit(solution)/shard_map/all_to_all | solution.py:96
  61.2 0.4 score.1
  61.6 10.1 %all_to_all.24 = f32[8,1,512]{2,1,0:T(1,128)S(1)} all-to-all(f32[8,1,512]{2,1,0:T(1,128)S(1)} %copy.14), channel_id=1, replica_groups=mesh['x'=4,'yl'=4,'c'=2,'yh'=2,'z'=8] {'z'}, dimensions={0} | all-to-all | bytes 32768 | tf_op jit(solution)/shard_map/all_to_all | solution.py:98
  71.7 0.6 reduce_sum.19
  (1 shorter events, 0.0 us)
Async XLA Ops:
  1.4 13.6 %all-to-all-start = ((bf16[8,16,512]{2,1,0:T(8,128)(2,1)}), bf16[8,16,512]{2,1,0:T(8,128)(2,1)S(1)}, u32[]{:S(2)}, u32[]{:S(2)}) async-start(bf16[8,16,512]{2,1,0:T(8,128)(2,1)} %broadcast_in_dim.4), calls=%async_computation | async-start | bytes 262144 | tf_op jit(solution)/shard_map/all_to_all | solution.py:89
  15.0 32.5 %all-to-all-start.1 = ((bf16[16,64,256]{2,1,0:T(8,128)(2,1)}), bf16[16,64,256]{2,1,0:T(8,128)(2,1)S(1)}, u32[]{:S(2)}, u32[]{:S(2)}) async-start(bf16[16,64,256]{2,1,0:T(8,128)(2,1)} %project.1), calls=%async_computation.1 | async-start | bytes 1048576 | tf_op jit(solution)/shard_map/all_to_all | solution.py:92
  29.6 23.8 %collective-permute-start.2 = (bf16[2,2,4,16,512]{4,3,2,1,0:T(8,128)(2,1)S(1)}, bf16[2,2,4,16,512]{4,3,2,1,0:T(8,128)(2,1)S(1)}, u32[]{:S(2)}, u32[]{:S(2)}) collective-permute-start(bf16[2,2,4,16,512]{4,3,2,1,0:T(8,128)(2,1)S(1)} %bitcast.8), channel_id=1, source_target_pairs={{0,384},{128,0},{256,128},{384,256},{1,385},{129,1},{257,129},{385... | collective-permute-start | bytes 786440 | tf_op jit(solution)/shard_map/ppermute | solution.py:94
  32.3 21.1 %collective-permute-start.1 = (bf16[2,2,4,16,512]{4,3,2,1,0:T(8,128)(2,1)S(1)}, bf16[2,2,4,16,512]{4,3,2,1,0:T(8,128)(2,1)S(1)}, u32[]{:S(2)}, u32[]{:S(2)}) collective-permute-start(bf16[2,2,4,16,512]{4,3,2,1,0:T(8,128)(2,1)S(1)} %bitcast.9), channel_id=1, source_target_pairs={{0,256},{128,384},{256,0},{384,128},{1,257},{129,385},{257,1},{385... | collective-permute-start | bytes 786440 | tf_op jit(solution)/shard_map/ppermute | solution.py:94
  35.3 18.1 %collective-permute-start = (bf16[2,2,4,16,512]{4,3,2,1,0:T(8,128)(2,1)S(1)}, bf16[2,2,4,16,512]{4,3,2,1,0:T(8,128)(2,1)S(1)}, u32[]{:S(2)}, u32[]{:S(2)}) collective-permute-start(bf16[2,2,4,16,512]{4,3,2,1,0:T(8,128)(2,1)S(1)} %bitcast.10), channel_id=1, source_target_pairs={{0,128},{128,256},{256,384},{384,0},{1,129},{129,257},{257,385},{3... | collective-permute-start | bytes 786440 | tf_op jit(solution)/shard_map/ppermute | solution.py:94
  48.9 12.2 %all-to-all-start.2 = ((bf16[8,2,512]{2,1,0:T(2,128)(2,1)}), bf16[8,2,512]{2,1,0:T(2,128)(2,1)S(1)}, u32[]{:S(2)}, u32[]{:S(2)}) async-start(bf16[8,2,512]{2,1,0:T(2,128)(2,1)} %pad_maximum_fusion), calls=%async_computation.2 | async-start | bytes 32768 | tf_op jit(solution)/shard_map/all_to_all | solution.py:96

commit v3 on v2

--- a/solution.py
+++ b/solution.py
@@ -62,20 +62,28 @@
 def score_kernel(sketch, *refs):
     pieces, out = refs[:-1], refs[-1]
     me = lax.axis_index("x")
-    for k, piece in enumerate(pieces):
+    totals = []
+    for piece in pieces:
         total = None
         for l in range(2):
-            rows = jnp.concatenate([piece[c, l, y] for y in range(4) for c in range(2)], axis=0)
+            rows = jnp.concatenate([piece[l, y] for y in range(4)], axis=0)
             part = lax.dot_general(sketch[:, l, :], rows, (((1,), (1,)), ((), ())), preferred_element_type=F32)
             total = part if total is None else total + part
-        at = lax.rem(me + 4 - k, 4) * 128
-        out[:, pl.ds(pl.multiple_of(at, 128), 128)] = total
+        totals.append(total)
+    slots = []
+    for x in range(4):
+        away = lax.rem(me + 4 - x, 4)
+        slot = totals[3]
+        for k in range(3):
+            slot = jnp.where(away == k, totals[k], slot)
+        slots.append(slot)
+    out[...] = jnp.concatenate(slots, axis=1)
 
 
 def score(sketch, pieces):
     return pl.pallas_call(
         score_kernel,
-        out_shape=jax.ShapeDtypeStruct((8, 512), F32),
+        out_shape=jax.ShapeDtypeStruct((16, 256), F32),
         in_specs=[WHOLE] * (1 + len(pieces)),
         out_specs=WHOLE,
         compiler_params=pltpu.CompilerParams(vmem_limit_bytes=16 << 20),
@@ -90,13 +98,15 @@
     projected = project((layer_input, up_grad, hidden, down_grad), (first_in, first_out, second_in, second_out))
     projected, q = lax.optimization_barrier((projected, q))
     shares = lax.all_to_all(projected, T, 0, 0, tiled=True)
-    q = lax.all_gather(q, "c", axis=0)
     pieces = [q] + [lax.ppermute(q, "x", [(i, (i + k) % 4) for i in range(4)]) for k in (1, 3, 2)]
     pieces = [pieces[0], pieces[1], pieces[3], pieces[2]]
-    sketch = lax.all_to_all(sketches(shares), "z", 0, 0, tiled=True)
+    sketch = sketches(shares)
+    sketch = jnp.concatenate([sketch, sketch], axis=0)
+    sketch = lax.all_to_all(sketch, ("c", "z"), 0, 0, tiled=True)
     part = score(sketch, pieces)
-    part = lax.all_to_all(part, "z", 0, 0, tiled=True)
-    return jnp.sum(part, axis=0, keepdims=True)
+    part = lax.all_to_all(part, ("c", "z"), 0, 0, tiled=True)
+    row = jnp.sum(part.reshape(2, 8, 256), axis=1)
+    return jnp.transpose(row.reshape(2, 16, rows), (1, 0, 2)).reshape(1, 32 * rows)
 
 
 def solution(mesh):

time: 72.9 us -> 73 us (level)
  blocking collectives: 12.1 us -> 10.1 us
  waiting for transfers between devices: 17.9 us -> 19.8 us
  local copies, waits for them, and re-layouts: 1.59 us -> 2.37 us
    all_gather x1 -> x0, blocking collectives: 1.99 us -> none  [local(): q = lax.all_gather(q, 'c', axis=0)]
    all_to_all x1, waiting for transfers between devices: 8.19 us -> 10.2 us  [local(): shares = lax.all_to_all(projected, T, 0, 0, tiled=True)]
    reshape x0 -> x2, local copies, waits for them, and re-layouts: none -> 0.75 us  [the longest x1 0.67 us: local(): jnp.transpose(row.reshape(2, 16, rows), (1, 0, 2)).reshape(1, 32 * rows)]
where the time goes in v3:
time: 73 us; the launch traced here: 72.5 us
  starting transfers between devices  34.3 us (47%)
  waiting for transfers between devices  19.8 us (27%)
  blocking collectives  10.1 us (14%)
  Pallas kernels  4.51 us (6%)
  local copies, waits for them, and re-layouts  2.37 us (3%)
  other arithmetic  0.78 us (1%)
    all_to_all x1, starting transfers between devices, local(): shares = lax.all_to_all(projected, T, 0, 0, tiled=True)  12.6 us
    all_to_all x1, waiting for transfers between devices, local(): shares = lax.all_to_all(projected, T, 0, 0, tiled=True)  10.2 us
    all_to_all x1, blocking collectives, local(): part = lax.all_to_all(part, ('c', 'z'), 0, 0, tiled=True)  10.1 us
    ppermute x3, starting transfers between devices, local(): lax.ppermute(q, 'x', [(i, (i + k) % 4) for i in range(4)])  9.76 us
    all_to_all x1, waiting for transfers between devices, local(): sketch = lax.all_to_all(sketch, ('c', 'z'), 0, 0, tiled=True)  7.66 us
    all_to_all x1, starting transfers between devices, local(): lax.all_to_all(copies, ('yh', 'yl'), 0, 0, tiled=True)  7.43 us
    all_to_all x1, starting transfers between devices, local(): sketch = lax.all_to_all(sketch, ('c', 'z'), 0, 0, tiled=True)  4.56 us
    pallas_call x1, Pallas kernels, project(): pl.pallas_call(project_kernel, out_shape=jax.ShapeDtypeStruct((16, LEN, 4...  4.2 us
  transfers between devices with their start and end apart: 6, of which 3 were waited for; matrix products, arithmetic and copies ran while one was open for 2% of the time, Pallas kernels for 6%

profile of v3, /device:TPU:22, one launch (start us, length us, event | category | flops | bytes accessed | tf_op | source)
XLA Modules:
  0.0 72.5 jit_solution(484247541497736535)
XLA Ops:
  0.0 1.4 %broadcast_in_dim.2 = bf16[8,16,512]{2,1,0:T(8,128)(2,1)} broadcast(bf16[16,512]{1,0:T(8,128)(2,1)} %param.17), dimensions={1,2} | broadcast | bytes 147456 | tf_op jit(solution)/shard_map/broadcast_in_dim | solution.py:96
  1.4 7.4 %all-to-all-start = ((bf16[8,16,512]{2,1,0:T(8,128)(2,1)}), bf16[8,16,512]{2,1,0:T(8,128)(2,1)S(1)}, u32[]{:S(2)}, u32[]{:S(2)}) async-start(bf16[8,16,512]{2,1,0:T(8,128)(2,1)} %broadcast_in_dim.2), calls=%async_computation | async-start | bytes 262144 | tf_op jit(solution)/shard_map/all_to_all | solution.py:97
  8.8 4.2 %project.1 = bf16[16,64,256]{2,1,0:T(8,128)(2,1)} custom-call(bf16[1024,256]{1,0:T(8,128)(2,1)} %x0.1, bf16[1024,896]{1,0:T(8,128)(2,1)} %x1.1, bf16[1024,896]{1,0:T(8,128)(2,1)} %x2.1, bf16[1024,256]{1,0:T(8,128)(2,1)} %x3.1, bf16[64,256]{1,0:T(8,128)(2,1)} %bitcast.17, bf16[64,896]{1,0:T(8,128)(2,1)} %bitcast.14, bf16[64,896]{1,0:T(8,128)(2,1)} %bitcast.15, ...), custom_call_target="tpu_custom_call" | custom-call | tf_op jit(solution)/shard_map/project/pallas_call | solution.py:37
  13.0 2.0 %all-to-all-done = bf16[8,16,512]{2,1,0:T(8,128)(2,1)S(1)} async-done(((bf16[8,16,512]{2,1,0:T(8,128)(2,1)}), bf16[8,16,512]{2,1,0:T(8,128)(2,1)S(1)}, u32[]{:S(2)}, u32[]{:S(2)}) %all-to-all-start) | async-done | bytes 131104 | tf_op jit(solution)/shard_map/all_to_all | solution.py:97
  15.0 12.6 %all-to-all-start.1 = ((bf16[16,64,256]{2,1,0:T(8,128)(2,1)}), bf16[16,64,256]{2,1,0:T(8,128)(2,1)S(1)}, u32[]{:S(2)}, u32[]{:S(2)}) async-start(bf16[16,64,256]{2,1,0:T(8,128)(2,1)} %project.1), calls=%async_computation.1 | async-start | bytes 1048576 | tf_op jit(solution)/shard_map/all_to_all | solution.py:100
  27.6 2.7 %collective-permute-start.2 = (bf16[2,4,16,512]{3,2,1,0:T(8,128)(2,1)S(1)}, bf16[2,4,16,512]{3,2,1,0:T(8,128)(2,1)S(1)}, u32[]{:S(2)}, u32[]{:S(2)}) collective-permute-start(bf16[2,4,16,512]{3,2,1,0:T(8,128)(2,1)S(1)} %bitcast.9), channel_id=1, source_target_pairs={{0,384},{128,0},{256,128},{384,256},{1,385},{129,1},{257,129},{385... | collective-permute-start | bytes 393224 | tf_op jit(solution)/shard_map/ppermute | solution.py:101
  30.3 3.0 %collective-permute-start.1 = (bf16[2,4,16,512]{3,2,1,0:T(8,128)(2,1)S(1)}, bf16[2,4,16,512]{3,2,1,0:T(8,128)(2,1)S(1)}, u32[]{:S(2)}, u32[]{:S(2)}) collective-permute-start(bf16[2,4,16,512]{3,2,1,0:T(8,128)(2,1)S(1)} %bitcast.10), channel_id=1, source_target_pairs={{0,256},{128,384},{256,0},{384,128},{1,257},{129,385},{257,1},{385... | collective-permute-start | bytes 393224 | tf_op jit(solution)/shard_map/ppermute | solution.py:101
  33.4 4.0 %collective-permute-start = (bf16[2,4,16,512]{3,2,1,0:T(8,128)(2,1)S(1)}, bf16[2,4,16,512]{3,2,1,0:T(8,128)(2,1)S(1)}, u32[]{:S(2)}, u32[]{:S(2)}) collective-permute-start(bf16[2,4,16,512]{3,2,1,0:T(8,128)(2,1)S(1)} %bitcast.11), channel_id=1, source_target_pairs={{0,128},{128,256},{256,384},{384,0},{1,129},{129,257},{257,385},{3... | collective-permute-start | bytes 393224 | tf_op jit(solution)/shard_map/ppermute | solution.py:101
  37.4 10.2 %all-to-all-done.1 = bf16[16,64,256]{2,1,0:T(8,128)(2,1)S(1)} async-done(((bf16[16,64,256]{2,1,0:T(8,128)(2,1)}), bf16[16,64,256]{2,1,0:T(8,128)(2,1)S(1)}, u32[]{:S(2)}, u32[]{:S(2)}) %all-to-all-start.1) | async-done | bytes 524320 | tf_op jit(solution)/shard_map/all_to_all | solution.py:100
  47.5 0.1 convert_reduce_fusion
  47.6 0.2 convolution_convert_fusion.1
  47.9 0.2 convolution_convert_fusion
  48.1 0.1 stack_reshape.9
  48.2 0.1 stack_reshape.8
  48.3 0.7 maximum_maximum_fusion
  49.0 4.6 %all-to-all-start.2 = ((bf16[16,2,512]{2,1,0:T(2,128)(2,1)}), bf16[16,2,512]{2,1,0:T(2,128)(2,1)S(1)}, u32[]{:S(2)}, u32[]{:S(2)}) async-start(bf16[16,2,512]{2,1,0:T(2,128)(2,1)} %maximum_maximum_fusion), calls=%async_computation.2 | async-start | bytes 65536 | tf_op jit(solution)/shard_map/all_to_all | solution.py:105
  53.6 0.0 collective-permute-done.2.refs_3_
  53.6 0.0 collective-permute-done.1.refs_2_
  53.6 0.0 collective-permute-done.refs_1_
  53.6 7.7 %all-to-all-done.2.sketch = bf16[16,2,512]{2,1,0:T(2,128)(2,1)S(1)} async-done(((bf16[16,2,512]{2,1,0:T(2,128)(2,1)}), bf16[16,2,512]{2,1,0:T(2,128)(2,1)S(1)}, u32[]{:S(2)}, u32[]{:S(2)}) %all-to-all-start.2) | async-done | bytes 32800 | tf_op jit(solution)/shard_map/all_to_all | solution.py:105
  61.2 0.3 score.1
  61.6 0.1 copy.17
  61.6 10.1 %all_to_all.24 = f32[16,1,256]{2,1,0:T(1,128)S(1)} all-to-all(f32[16,1,256]{2,1,0:T(1,128)S(1)} %copy.17), channel_id=1, replica_groups=mesh['x'=4,'yl'=4,'c'=2,'yh'=2,'z'=8] {'c','z'}, dimensions={0} | all-to-all | bytes 32768 | tf_op jit(solution)/shard_map/all_to_all | solution.py:107
  71.8 0.1 reshape.18
  71.9 0.7 reshape.19
  (2 shorter events, 0.0 us)
Async XLA Ops:
  1.4 13.6 %all-to-all-start = ((bf16[8,16,512]{2,1,0:T(8,128)(2,1)}), bf16[8,16,512]{2,1,0:T(8,128)(2,1)S(1)}, u32[]{:S(2)}, u32[]{:S(2)}) async-start(bf16[8,16,512]{2,1,0:T(8,128)(2,1)} %broadcast_in_dim.2), calls=%async_computation | async-start | bytes 262144 | tf_op jit(solution)/shard_map/all_to_all | solution.py:97
  15.0 32.5 %all-to-all-start.1 = ((bf16[16,64,256]{2,1,0:T(8,128)(2,1)}), bf16[16,64,256]{2,1,0:T(8,128)(2,1)S(1)}, u32[]{:S(2)}, u32[]{:S(2)}) async-start(bf16[16,64,256]{2,1,0:T(8,128)(2,1)} %project.1), calls=%async_computation.1 | async-start | bytes 1048576 | tf_op jit(solution)/shard_map/all_to_all | solution.py:100
  27.6 26.0 %collective-permute-start.2 = (bf16[2,4,16,512]{3,2,1,0:T(8,128)(2,1)S(1)}, bf16[2,4,16,512]{3,2,1,0:T(8,128)(2,1)S(1)}, u32[]{:S(2)}, u32[]{:S(2)}) collective-permute-start(bf16[2,4,16,512]{3,2,1,0:T(8,128)(2,1)S(1)} %bitcast.9), channel_id=1, source_target_pairs={{0,384},{128,0},{256,128},{384,256},{1,385},{129,1},{257,129},{385... | collective-permute-start | bytes 393224 | tf_op jit(solution)/shard_map/ppermute | solution.py:101
  30.3 23.2 %collective-permute-start.1 = (bf16[2,4,16,512]{3,2,1,0:T(8,128)(2,1)S(1)}, bf16[2,4,16,512]{3,2,1,0:T(8,128)(2,1)S(1)}, u32[]{:S(2)}, u32[]{:S(2)}) collective-permute-start(bf16[2,4,16,512]{3,2,1,0:T(8,128)(2,1)S(1)} %bitcast.10), channel_id=1, source_target_pairs={{0,256},{128,384},{256,0},{384,128},{1,257},{129,385},{257,1},{385... | collective-permute-start | bytes 393224 | tf_op jit(solution)/shard_map/ppermute | solution.py:101
  33.4 20.2 %collective-permute-start = (bf16[2,4,16,512]{3,2,1,0:T(8,128)(2,1)S(1)}, bf16[2,4,16,512]{3,2,1,0:T(8,128)(2,1)S(1)}, u32[]{:S(2)}, u32[]{:S(2)}) collective-permute-start(bf16[2,4,16,512]{3,2,1,0:T(8,128)(2,1)S(1)} %bitcast.11), channel_id=1, source_target_pairs={{0,128},{128,256},{256,384},{384,0},{1,129},{129,257},{257,385},{3... | collective-permute-start | bytes 393224 | tf_op jit(solution)/shard_map/ppermute | solution.py:101
  49.0 12.3 %all-to-all-start.2 = ((bf16[16,2,512]{2,1,0:T(2,128)(2,1)}), bf16[16,2,512]{2,1,0:T(2,128)(2,1)S(1)}, u32[]{:S(2)}, u32[]{:S(2)}) async-start(bf16[16,2,512]{2,1,0:T(2,128)(2,1)} %maximum_maximum_fusion), calls=%async_computation.2 | async-start | bytes 65536 | tf_op jit(solution)/shard_map/all_to_all | solution.py:105

commit v4 on v3

--- a/solution.py
+++ b/solution.py
@@ -59,24 +59,15 @@
     )
 
 
-def score_kernel(sketch, *refs):
-    pieces, out = refs[:-1], refs[-1]
-    me = lax.axis_index("x")
-    totals = []
-    for piece in pieces:
+def score_kernel(sketch, q, out):
+    slots = []
+    for x in range(4):
         total = None
         for l in range(2):
-            rows = jnp.concatenate([piece[l, y] for y in range(4)], axis=0)
+            rows = jnp.concatenate([q[x, l, y] for y in range(4)], axis=0)
             part = lax.dot_general(sketch[:, l, :], rows, (((1,), (1,)), ((), ())), preferred_element_type=F32)
             total = part if total is None else total + part
-        totals.append(total)
-    slots = []
-    for x in range(4):
-        away = lax.rem(me + 4 - x, 4)
-        slot = totals[3]
-        for k in range(3):
-            slot = jnp.where(away == k, totals[k], slot)
-        slots.append(slot)
+        slots.append(total)
     out[...] = jnp.concatenate(slots, axis=1)
 
 
@@ -98,8 +89,8 @@
     projected = project((layer_input, up_grad, hidden, down_grad), (first_in, first_out, second_in, second_out))
     projected, q = lax.optimization_barrier((projected, q))
     shares = lax.all_to_all(projected, T, 0, 0, tiled=True)
-    pieces = [q] + [lax.ppermute(q, "x", [(i, (i + k) % 4) for i in range(4)]) for k in (1, 3, 2)]
-    pieces = [pieces[0], pieces[1], pieces[3], pieces[2]]
+    pieces = [lax.all_gather(q, "x", axis=0)]
+    shares, pieces = lax.optimization_barrier((shares, pieces))
     sketch = sketches(shares)
     sketch = jnp.concatenate([sketch, sketch], axis=0)
     sketch = lax.all_to_all(sketch, ("c", "z"), 0, 0, tiled=True)

time: 73 us -> 72.2 us (0.989)
  blocking collectives: 10.1 us -> 35.2 us
  starting transfers between devices: 34.3 us -> 20 us
  waiting for transfers between devices: 19.8 us -> 8.89 us
    all_gather x0 -> x1, blocking collectives: none -> 13.1 us  [local(): pieces = [lax.all_gather(q, 'x', axis=0)]]
    all_to_all x0 -> x1, blocking collectives: none -> 12 us  [local(): sketch = lax.all_to_all(sketch, ('c', 'z'), 0, 0, tiled=True)]
    ppermute x3 -> x0, starting transfers between devices: 9.76 us -> none  [local(): lax.ppermute(q, 'x', [(i, (i + k) % 4) for i in range(4)])]
    all_to_all x1 -> x0, waiting for transfers between devices: 7.66 us -> none  [local(): sketch = lax.all_to_all(sketch, ('c', 'z'), 0, 0, tiled=True)]
    all_to_all x1 -> x0, starting transfers between devices: 4.56 us -> none  [local(): sketch = lax.all_to_all(sketch, ('c', 'z'), 0, 0, tiled=True)]
    all_to_all x1, waiting for transfers between devices: 10.2 us -> 6.9 us  [local(): shares = lax.all_to_all(projected, T, 0, 0, tiled=True)]
  transfers between devices with their start and end apart: 6 -> 2, of which waited for: 3 -> 2; matrix products, arithmetic and copies ran while one was open for 2% -> 0% of each run, Pallas kernels for 6% -> 6%
where the time goes in v4:
time: 72.2 us; the launch traced here: 71.7 us
  blocking collectives  35.2 us (49%)
  starting transfers between devices  20 us (28%)
  waiting for transfers between devices  8.89 us (12%)
  Pallas kernels  4.49 us (6%)
  local copies, waits for them, and re-layouts  2.4 us (3%)
    all_gather x1, blocking collectives, local(): pieces = [lax.all_gather(q, 'x', axis=0)]  13.1 us
    all_to_all x1, starting transfers between devices, local(): shares = lax.all_to_all(projected, T, 0, 0, tiled=True)  12.6 us
    all_to_all x1, blocking collectives, local(): sketch = lax.all_to_all(sketch, ('c', 'z'), 0, 0, tiled=True)  12 us
    all_to_all x1, blocking collectives, local(): part = lax.all_to_all(part, ('c', 'z'), 0, 0, tiled=True)  10.1 us
    all_to_all x1, starting transfers between devices, local(): lax.all_to_all(copies, ('yh', 'yl'), 0, 0, tiled=True)  7.43 us
    all_to_all x1, waiting for transfers between devices, local(): shares = lax.all_to_all(projected, T, 0, 0, tiled=True)  6.9 us
    pallas_call x1, Pallas kernels, project(): pl.pallas_call(project_kernel, out_shape=jax.ShapeDtypeStruct((16, LEN, 4...  4.2 us
    all_to_all x1, waiting for transfers between devices, local(): lax.all_to_all(copies, ('yh', 'yl'), 0, 0, tiled=True)  1.99 us
  transfers between devices with their start and end apart: 2, of which 2 were waited for; matrix products, arithmetic and copies ran while one was open for 0% of the time, Pallas kernels for 6%

profile of v4, /device:TPU:22, one launch (start us, length us, event | category | flops | bytes accessed | tf_op | source)
XLA Modules:
  0.0 71.7 jit_solution(8045548077066742400)
XLA Ops:
  0.0 1.4 %broadcast_in_dim.2 = bf16[8,16,512]{2,1,0:T(8,128)(2,1)} broadcast(bf16[16,512]{1,0:T(8,128)(2,1)} %param.17), dimensions={1,2} | broadcast | bytes 147456 | tf_op jit(solution)/shard_map/broadcast_in_dim | solution.py:87
  1.4 7.4 %all-to-all-start = ((bf16[8,16,512]{2,1,0:T(8,128)(2,1)}), bf16[8,16,512]{2,1,0:T(8,128)(2,1)S(1)}, u32[]{:S(2)}, u32[]{:S(2)}) async-start(bf16[8,16,512]{2,1,0:T(8,128)(2,1)} %broadcast_in_dim.2), calls=%async_computation | async-start | bytes 262144 | tf_op jit(solution)/shard_map/all_to_all | solution.py:88
  8.8 4.2 %project.1 = bf16[16,64,256]{2,1,0:T(8,128)(2,1)} custom-call(bf16[1024,256]{1,0:T(8,128)(2,1)} %x0.1, bf16[1024,896]{1,0:T(8,128)(2,1)} %x1.1, bf16[1024,896]{1,0:T(8,128)(2,1)} %x2.1, bf16[1024,256]{1,0:T(8,128)(2,1)} %x3.1, bf16[64,256]{1,0:T(8,128)(2,1)} %bitcast.16, bf16[64,896]{1,0:T(8,128)(2,1)} %bitcast.13, bf16[64,896]{1,0:T(8,128)(2,1)} %bitcast.14, ...), custom_call_target="tpu_custom_call" | custom-call | tf_op jit(solution)/shard_map/project/pallas_call | solution.py:37
  13.0 2.0 %all-to-all-done = bf16[8,16,512]{2,1,0:T(8,128)(2,1)S(1)} async-done(((bf16[8,16,512]{2,1,0:T(8,128)(2,1)}), bf16[8,16,512]{2,1,0:T(8,128)(2,1)S(1)}, u32[]{:S(2)}, u32[]{:S(2)}) %all-to-all-start) | async-done | bytes 131104 | tf_op jit(solution)/shard_map/all_to_all | solution.py:88
  15.0 12.6 %all-to-all-start.1 = ((bf16[16,64,256]{2,1,0:T(8,128)(2,1)}), bf16[16,64,256]{2,1,0:T(8,128)(2,1)S(1)}, u32[]{:S(2)}, u32[]{:S(2)}) async-start(bf16[16,64,256]{2,1,0:T(8,128)(2,1)} %project.1), calls=%async_computation.1 | async-start | bytes 1048576 | tf_op jit(solution)/shard_map/all_to_all | solution.py:91
  27.6 13.1 %all-gather = bf16[8,4,16,512]{3,2,1,0:T(8,128)(2,1)S(1)} all-gather(bf16[2,4,16,512]{3,2,1,0:T(8,128)(2,1)S(1)} %bitcast.12), channel_id=2, replica_groups=mesh['x'=4,'yl'=4,'c'=2,'yh'=2,'z'=8] {'x'}, dimensions={0}, use_global_device_ids=true | all-gather | bytes 655360 | tf_op jit(solution)/shard_map/all_gather | solution.py:92
  40.7 6.9 %all-to-all-done.1 = bf16[16,64,256]{2,1,0:T(8,128)(2,1)S(1)} async-done(((bf16[16,64,256]{2,1,0:T(8,128)(2,1)}), bf16[16,64,256]{2,1,0:T(8,128)(2,1)S(1)}, u32[]{:S(2)}, u32[]{:S(2)}) %all-to-all-start.1) | async-done | bytes 524320 | tf_op jit(solution)/shard_map/all_to_all | solution.py:91
  47.6 0.1 convert_reduce_fusion
  47.6 0.2 convolution_convert_fusion.1
  47.9 0.2 convolution_convert_fusion
  48.1 0.1 stack_reshape.9
  48.2 0.1 stack_reshape.8
  48.3 0.1 maximum_maximum_fusion
  48.4 12.0 %all_to_all.24.sketch = bf16[16,2,512]{2,1,0:T(2,128)(2,1)S(1)} all-to-all(bf16[16,2,512]{2,1,0:T(2,128)(2,1)S(1)} %maximum_maximum_fusion), channel_id=1, replica_groups=mesh['x'=4,'yl'=4,'c'=2,'yh'=2,'z'=8] {'c','z'}, dimensions={0} | all-to-all | bytes 65536 | tf_op jit(solution)/shard_map/all_to_all | solution.py:96
  60.5 0.3 score.1
  60.7 0.1 copy.17
  60.8 10.1 %all_to_all.25 = f32[16,1,256]{2,1,0:T(1,128)S(1)} all-to-all(f32[16,1,256]{2,1,0:T(1,128)S(1)} %copy.17), channel_id=1, replica_groups=mesh['x'=4,'yl'=4,'c'=2,'yh'=2,'z'=8] {'c','z'}, dimensions={0} | all-to-all | bytes 32768 | tf_op jit(solution)/shard_map/all_to_all | solution.py:98
  71.0 0.1 reshape.18
  71.1 0.7 reshape.19
  (2 shorter events, 0.0 us)
Async XLA Ops:
  1.4 13.6 %all-to-all-start = ((bf16[8,16,512]{2,1,0:T(8,128)(2,1)}), bf16[8,16,512]{2,1,0:T(8,128)(2,1)S(1)}, u32[]{:S(2)}, u32[]{:S(2)}) async-start(bf16[8,16,512]{2,1,0:T(8,128)(2,1)} %broadcast_in_dim.2), calls=%async_computation | async-start | bytes 262144 | tf_op jit(solution)/shard_map/all_to_all | solution.py:88
  15.0 32.6 %all-to-all-start.1 = ((bf16[16,64,256]{2,1,0:T(8,128)(2,1)}), bf16[16,64,256]{2,1,0:T(8,128)(2,1)S(1)}, u32[]{:S(2)}, u32[]{:S(2)}) async-start(bf16[16,64,256]{2,1,0:T(8,128)(2,1)} %project.1), calls=%async_computation.1 | async-start | bytes 1048576 | tf_op jit(solution)/shard_map/all_to_all | solution.py:91
